TPU v7x, 128 devices: a whole 4x4x4 slice. The times are simulated.
128 devices in a mesh: group: 4 (over y), col: 32 (over z, x, core).
Axes of the slice: x: 4, y: 4, z: 4, core: 2. Of those that a mesh axis runs over, the one named last changes fastest.
Arguments:
- layer_input: bfloat16 [16384, 4096], P(('group', 'col')), may hold values from -6 to 6
- norm_gain: bfloat16 [4096], replicated, may hold values from 0.099609375 to 1.8984375
- keyvalue_cotangent: bfloat16 [16384, 2048], P(('group', 'col')), may hold values from -6 to 6
- keyvalue_weight: bfloat16 [4096, 2048], P('col'), may hold values from -0.125 to 0.125
- residual_cotangent: bfloat16 [16384, 4096], P(('group', 'col')), may hold values from -6 to 6
- ngram_ids: int32 [16384, 2], P(('group', 'col')), may hold values from 0 to 32767, as said below
- table: float32 [32768, 4096], P('group', 'col'), may hold values from -6 to 6
- accumulator: float32 [32768], P('group'), may hold values from 0.05 to 2
Outputs:
- new_table: float32 [32768, 4096], P('group', 'col')
- new_accum: float32 [32768], P('group')
Inputs may be any that keep to these rules, and one draw needn't show every extreme that they name: `ngram_ids`: row r belongs to owner group r // 8192. Among the 256 entries of one device's tokens (aligned blocks of 128 tokens), at most 128 belong to any one owner group, and one owner group, the same for every device, holds exactly 128 of them.
All inputs are finite; a program needn't handle non-finite values.
Results may differ from a plain program's by a relative error of at most 0.0009.
Values may be sent and summed in bfloat16 or wider, within the bound.
No kernel may reach another device: no remote copies, remote signals or barrier semaphores. Data moves between devices by JAX's collectives and lax.ppermute only.
A program may use at most 128 MiB of HBM per device.

v0:
```python
import functools

import jax
import jax.numpy as jnp
from jax import lax
from jax.experimental import pallas as pl
from jax.experimental.pallas import tpu as pltpu
from jax.sharding import PartitionSpec as P

NGRAM = 2
R_GRP = 8192
PAD = 8
VMEM_LIMIT = 56 * 1024 * 1024
learn_rate = 0.5

NT = (((1,), (1,)), ((), ()))
NN = (((1,), (0,)), ((), ()))


def slots_of(ngram_ids, groups):
    tok = ngram_ids.shape[0]
    ids = ngram_ids.reshape(-1)
    n = ids.shape[0]
    order = jnp.arange(n, dtype=jnp.int32)
    same = ids[:, None] == ids[None, :]
    leader = jnp.min(jnp.where(same, order[None, :], n), axis=1)
    lead = leader == order
    owner = ids // R_GRP
    before = lead[None, :] & (owner[:, None] == owner[None, :]) & (order[None, :] < leader[:, None])
    slot = jnp.sum(before.astype(jnp.int32), axis=1)
    places = jnp.arange(groups * tok, dtype=jnp.int32)
    rows = jnp.min(
        jnp.where(
            places[:, None] == (owner * tok + slot)[None, :], (ids - owner * R_GRP)[None, :], R_GRP
        ),
        axis=1,
    )
    mine = owner[None, :] == jnp.arange(groups, dtype=jnp.int32)[:, None]
    maps = jnp.where(mine, slot[None, :], -1).reshape(groups, tok, NGRAM)
    parts = [rows.reshape(groups, tok)] + [maps[:, :, j] for j in range(NGRAM)]
    return jnp.concatenate(parts, axis=1)


def product_kernel(pieces, first, last, columns, *refs):
    n = len(pieces)
    where, refs = refs[0], refs[1:]
    cot_own, cot_pair = refs[0], refs[1]
    ws = refs[2 : 2 + n]
    tok, deep = cot_own.shape
    depth = deep // 2
    if first:
        v_own, v_pair, ng, ss = refs[2 + n :]
        ng[...] = jnp.zeros_like(ng)
    else:
        held, gain, v_own, v_pair, ng, inner = refs[2 + n :]
        ng[...] = held[...]
    lanes = ng.shape[3]
    for (half, blocks), w in zip(pieces, ws):
        at = slice(half * depth, (half + 1) * depth)
        for k in range(0, len(blocks), 2):
            rows = w[k * lanes : (k + 2) * lanes, :]
            for part, cot in enumerate((cot_own, cot_pair)):
                p = lax.dot_general(cot[:, at], rows, NT, preferred_element_type=jnp.float32)
                for j in range(2):
                    ng[blocks[k + j], part] += p[:, j * lanes : (j + 1) * lanes]
    if first:
        for part, v in enumerate((v_own, v_pair)):

            def squares(j, total):
                x = v[:, pl.ds(pl.multiple_of(j * lanes, lanes), lanes)].astype(jnp.float32)
                return total + x * x

            ss[part] = lax.fori_loop(0, columns, squares, jnp.zeros((tok, lanes), jnp.float32))
    if last:
        for part, v in enumerate((v_own, v_pair)):

            def products(j, total):
                at = pl.ds(pl.multiple_of(where[j] * lanes, lanes), lanes)
                scaled = ng[j, part] * gain[:, at].astype(jnp.float32)
                ng[j, part] = scaled
                return total + scaled * v[:, at].astype(jnp.float32)

            inner[part] = lax.fori_loop(
                0, ng.shape[0], products, jnp.zeros((tok, lanes), jnp.float32)
            )


def finish_kernel(width, where, ng, ss, inner, other, v_own, v_pair, r_own, r_pair, out):
    tok, lanes = ng.shape[2:]
    core = lax.rem(where[0], 2)
    for part, (v, r) in enumerate(((v_own, r_own), (v_pair, r_pair))):
        square = jnp.sum(ss[part], axis=1, keepdims=True)
        inverse = lax.rsqrt(square / width + 1e-05)
        cubed = inverse * inverse * inverse
        mean = jnp.sum(inner[part] + other[1 - part], axis=1, keepdims=True) / width
        place = core if part == 0 else 1 - core

        def block(j, carry):
            at = pl.ds(pl.multiple_of(where[j] * lanes, lanes), lanes)
            values = v[:, at].astype(jnp.float32)
            total = inverse * ng[j, part] - values * cubed * mean + r[:, at].astype(jnp.float32)
            out[lax.div(where[j], 2), place] = total.astype(out.dtype)
            return carry

        lax.fori_loop(0, ng.shape[0], block, 0)


def vmem_call(kernel, n, out_shape, name, aliases=None):
    space = pl.BlockSpec(memory_space=pltpu.VMEM)
    return pl.pallas_call(
        kernel,
        in_specs=[pl.BlockSpec(memory_space=pltpu.SMEM)] + [space] * (n - 1),
        out_specs=jax.tree.map(lambda _: space, out_shape),
        out_shape=out_shape,
        input_output_aliases=aliases or {},
        compiler_params=pltpu.CompilerParams(vmem_limit_bytes=40 * 1024 * 1024),
        name=name,
    )


def shifted(value, inner_size, size, by):
    pairs = []
    for d in range(lax.axis_size("col")):
        low, high = d % inner_size, d // inner_size
        mid, top = high % size, high // size
        pairs.append((d, (top * size + (mid + by) % size) * inner_size + low))
    return lax.ppermute(value, "col", pairs)


def along(x, axis):
    inner_size = {"x": 2, "z": 8}[axis]
    left, right = shifted(x, inner_size, 4, 1), shifted(x, inner_size, 4, 3)
    return left, right


def token_grads(cot, w, v, r, gain, lanes, plan):
    columns = lax.axis_size("col")
    tok, width = v.shape
    depth = w.shape[1] // 2
    me = lax.axis_index("col")
    z, x, core = me // 8, (me // 2) % 4, me % 2
    where = jnp.stack(
        [
            (((z + 4 - dz) % 4) * 4 + (x + 4 - dx) % 4) * 2 + core
            for dz in range(4)
            for dx in range(4)
        ]
    ).astype(jnp.int32)
    cot_pair, v_pair, r_pair = (shifted(t, 1, 2, 1) for t in (cot, v, r))
    step = {"x": 2, "z": 8}
    firsts = []
    for half, axis in enumerate("xz"):
        own = w[:, half * depth : (half + 1) * depth]
        firsts.append((own, *along(own, axis), shifted(own, step[axis], 4, 2)))
    lows = [jnp.concatenate([own, left]) for own, left, _, _ in firsts]
    highs = [jnp.concatenate([farther, right]) for _, _, right, farther in firsts]
    low_sides = [along(lows[0], "z"), along(lows[1], "x")]
    high_sides = [along(highs[0], "z"), along(highs[1], "x")]
    far = [
        (shifted(low_sides[half][0], step[axis], 4, 1), shifted(high_sides[half][1], step[axis], 4, 3))
        for half, axis in enumerate("zx")
    ]

    def line(half, k, low=0, high=4):
        return (half, [k * 4 + j if half == 0 else j * 4 + k for j in range(low, high)])

    pieces, ws = [], []
    for half in range(2):
        low_set = (lows[half], *low_sides[half])
        high_set = (highs[half], *high_sides[half])
        for k, low, high in zip((0, 1, 3), low_set, high_set):
            pieces += [line(half, k, 0, 2), line(half, k, 2, 4)]
            ws += [low, high]
    product = jax.ShapeDtypeStruct((16, 2, tok, lanes), jnp.float32)
    stat = jax.ShapeDtypeStruct((2, tok, lanes), jnp.float32)
    plan, cot = lax.optimization_barrier((plan, cot))
    args = (where, cot, cot_pair, *ws, v, v_pair)
    ng, ss = vmem_call(
        functools.partial(product_kernel, pieces, True, False, columns),
        len(args),
        (product, stat),
        "product_near",
    )(*args)
    pieces, ws = [], []
    for half in range(2):
        for low, piece in ((0, far[half][0]), (2, far[half][1])):
            pieces.append(line(half, 2, low, low + 2))
            ws.append(piece)
    args = (where, cot, cot_pair, *ws, ng, gain.reshape(1, width), v, v_pair)
    scaled, inner = vmem_call(
        functools.partial(product_kernel, pieces, False, True, columns),
        len(args),
        (product, stat),
        "product_far",
        {len(args) - 4: 0},
    )(*args)
    other = shifted(inner, 1, 2, 1)
    args = (where, scaled, ss, inner, other, v, v_pair, r, r_pair)
    grads = vmem_call(
        functools.partial(finish_kernel, width),
        len(args),
        jax.ShapeDtypeStruct((16, 2, tok, lanes), jnp.bfloat16),
        "token_grads",
    )(*args)
    return grads, plan


def scatter_kernel(first, parts, index, per, batch, rows, counts, *refs):
    i = pl.program_id(0)
    n = len(parts)
    xs, maps = refs[:n], refs[n]
    if first:
        grad = refs[n + 1]
    else:
        held, grad = refs[n + 1], refs[n + 2]
    wide = refs[-1]
    tok, lanes = wide.shape[1], wide.shape[2]

    @pl.when(i == 0)
    def _():
        grad[...] = jnp.zeros_like(grad) if first else held[...]

    place = lax.broadcasted_iota(jnp.int32, (tok, tok), 0)

    def merge(x):
        for k in range(per):
            total = (place == maps[k, 0:1, :]).astype(jnp.float32)
            for j in range(1, NGRAM):
                total += (place == maps[k, j : j + 1, :]).astype(jnp.float32)
            wide[k] = (
                lax.dot_general(
                    total.astype(jnp.bfloat16), x[k], NN, preferred_element_type=jnp.float32
                )
                .astype(jnp.bfloat16)
                .astype(jnp.float32)
            )

    start = 0
    for p in range(n):
        pl.when((i >= start) & (i < start + parts[p]))(functools.partial(merge, xs[p]))
        start += parts[p]

    def block(k, carry):
        b = index(i) * per + k

        def part(low, high):
            for base in range(low, high, batch):
                at = [rows[b * tok + base + s] for s in range(batch)]
                old = [grad[pl.ds(at[s], 1), :] for s in range(batch)]
                new = [old[s] + wide[k, pl.ds(base + s, 1), :] for s in range(batch)]
                for s in range(batch):
                    grad[pl.ds(at[s], 1), :] = new[s]

        part(0, tok // 2)

        @pl.when(counts[b] > tok // 2)
        def _():
            part(tok // 2, tok)

        return carry

    lax.fori_loop(0, per, block, 0)


def scattered(xs, maps, rows, counts, held, skips=(0, 0)):
    tok, lanes = xs[0].shape[1:]
    per = 16
    parts = [x.shape[0] // per for x in xs]
    starts = [sum(parts[:p]) for p in range(len(parts))]

    def index(i):
        return i + jnp.where(i < parts[0], skips[0], skips[1])

    def piece(p):
        return lambda i, *_: (jnp.clip(i - starts[p], 0, parts[p] - 1), 0, 0)

    total = (R_GRP + PAD, lanes)
    in_specs = [pl.BlockSpec((per, tok, lanes), piece(p)) for p in range(len(xs))]
    in_specs.append(pl.BlockSpec((per, NGRAM, tok), lambda i, *_: (index(i), 0, 0)))
    args = [rows.reshape(-1), counts, *xs, maps]
    stays = pl.BlockSpec(memory_space=pltpu.VMEM)
    if held is not None:
        in_specs.append(stays)
        args.append(held)
    return pl.pallas_call(
        functools.partial(scatter_kernel, held is None, parts, index, per, 16),
        grid_spec=pltpu.PrefetchScalarGridSpec(
            num_scalar_prefetch=2,
            grid=(sum(parts),),
            in_specs=in_specs,
            out_specs=stays,
            scratch_shapes=[pltpu.VMEM((per, tok, lanes), jnp.float32)],
        ),
        out_shape=jax.ShapeDtypeStruct(total, jnp.float32),
        input_output_aliases={} if held is None else {len(args) - 1: 0},
        compiler_params=pltpu.CompilerParams(
            dimension_semantics=("arbitrary",), vmem_limit_bytes=20 * 1024 * 1024
        ),
        cost_estimate=pl.CostEstimate(
            flops=1000000, bytes_accessed=900000 * sum(x.shape[0] for x in xs), transcendentals=0
        ),
        name="scatter_rows",
    )(*args)


def ring(x, by):
    n = lax.axis_size("group")
    return lax.ppermute(x, "group", [(d, (d + by) % n) for d in range(n)])


def col_sum(x):
    x = x + shifted(x, 1, 2, 1)
    for inner_size in (2, 8):
        first, second, third = (shifted(x, inner_size, 4, by) for by in (1, 3, 2))
        x = (x + third) + (first + second)
    return x


def shards(
    layer_input,
    norm_gain,
    keyvalue_cotangent,
    keyvalue_weight,
    residual_cotangent,
    ngram_ids,
    table,
    accumulator,
):
    groups, columns = lax.axis_size("group"), lax.axis_size("col")
    tok, width = layer_input.shape
    lanes = table.shape[1]
    def exchange(plan):
        sent = jnp.broadcast_to(plan[:, None, :], (groups, columns, plan.shape[1]))
        got = lax.all_to_all(
            sent.reshape(groups * columns, -1), ("group", "col"), 0, 0, tiled=True
        ).reshape(groups, columns, -1)
        me = lax.axis_index("group")
        order = [(me + by) % groups for by in (0, 3, 1, 2)]
        got = [lax.dynamic_index_in_dim(got, g, 0, False) for g in order]
        got = [got[0], jnp.concatenate(got[1:3]), got[3]]
        rows = [g[:, :tok] for g in got]
        maps = [g[:, tok:].reshape(-1, NGRAM, tok) for g in got]
        counts = [jnp.sum((r < R_GRP).astype(jnp.int32), axis=1) for r in rows]
        return rows, maps, counts

    grads, plan = token_grads(
        keyvalue_cotangent,
        keyvalue_weight,
        layer_input,
        residual_cotangent,
        norm_gain,
        lanes,
        slots_of(ngram_ids, groups),
    )
    planes = [[q * 2 + core for q in range(columns // 2)] for core in range(2)]
    own = lax.all_to_all(
        grads.reshape(columns // 2, 2 * tok, lanes),
        "col",
        0,
        0,
        axis_index_groups=planes,
        tiled=True,
    ).reshape(columns, tok, lanes)
    half = columns // 2
    low, high = own[:half], own[half:]
    low_left, high_right = ring(low, 1), ring(high, 3)
    high_left, low_right = ring(high, 1), ring(low, 3)
    rows, maps, counts = exchange(lax.optimization_barrier((plan, low, high))[0])
    grad = scattered((own,), maps[0], rows[0], counts[0], None)
    far = (ring(low_left, 1), ring(high_right, 3))
    quarter = half // 16
    first, then = (low_left, high_right), (high_left, low_right)
    grad = scattered(first, maps[1], rows[1], counts[1], grad, (0, 2 * quarter))
    grad = scattered(then, maps[1], rows[1], counts[1], grad, (quarter, quarter))
    grad = scattered(far, maps[2], rows[2], counts[2], grad)[:R_GRP]
    partial = jnp.sum(grad * grad, axis=1).reshape(-1, lanes)
    squares = col_sum(partial) / width
    new_accum = accumulator + squares.reshape(-1)
    new_table = table - learn_rate * grad * lax.rsqrt(new_accum)[:, None]
    return (new_table, new_accum)


def solution(mesh):
    in_specs = (
        P(("group", "col"), None),
        P(),
        P(("group", "col"), None),
        P("col", None),
        P(("group", "col"), None),
        P(("group", "col"), None),
        P("group", "col"),
        P("group"),
    )
    out_specs = (P("group", "col"), P("group"))
    return jax.shard_map(shards, mesh=mesh, in_specs=in_specs, out_specs=out_specs, check_vma=False)
```

profile of v0, /device:TPU:6, one launch (start us, length us, event | category | flops | bytes accessed | tf_op | source)
XLA Modules:
  0.0 177.8 jit_solution(15694022177153484678)
XLA Ops:
  1.8 4.0 %collective-permute-start.11 = (bf16[128,1024]{1,0:T(8,128)(2,1)S(1)}, bf16[128,1024]{1,0:T(8,128)(2,1)S(1)}, u32[]{:S(2)}, u32[]{:S(2)}) collective-permute-start(bf16[128,1024]{1,0:T(8,128)(2,1)S(1)} %get-tuple-element.22), channel_id=1, source_target_pairs={{0,16},{1,17},{2,18},{3,19},{4,20},{5,21},{6,22},{7,23},{8,24},{9,... | collective-permute-start | bytes 786440 | tf_op jit(solution)/shard_map/ppermute | solution.py:127
  7.9 3.2 %collective-permute-start.1 = (bf16[128,1024]{1,0:T(8,128)(2,1)S(1)}, bf16[128,1024]{1,0:T(8,128)(2,1)}, u32[]{:S(2)}, u32[]{:S(2)}) collective-permute-start(bf16[128,1024]{1,0:T(8,128)(2,1)S(1)} %get-tuple-element.23), channel_id=1, source_target_pairs={{0,2},{1,3},{2,4},{3,5},{4,6},{5,7},{6,0},{7,1},{8,10},{9,11},{10,... | collective-permute-start | bytes 786440 | tf_op jit(solution)/shard_map/ppermute | solution.py:127
  12.1 2.5 %collective-permute-start.8 = (bf16[128,1024]{1,0:T(8,128)(2,1)S(1)}, bf16[128,1024]{1,0:T(8,128)(2,1)S(1)}, u32[]{:S(2)}, u32[]{:S(2)}) collective-permute-start(bf16[128,1024]{1,0:T(8,128)(2,1)S(1)} %get-tuple-element.22), channel_id=1, source_target_pairs={{0,8},{1,9},{2,10},{3,11},{4,12},{5,13},{6,14},{7,15},{8,16},{9,17... | collective-permute-start | bytes 786440 | tf_op jit(solution)/shard_map/ppermute | solution.py:127
  21.4 2.0 %collective-permute-start.6 = (bf16[256,1024]{1,0:T(8,128)(2,1)}, bf16[256,1024]{1,0:T(8,128)(2,1)}, u32[]{:S(2)}, u32[]{:S(2)}) collective-permute-start(bf16[256,1024]{1,0:T(8,128)(2,1)} %constant_dynamic-update-slice_fusion.refs_4_), channel_id=1, source_target_pairs={{0,24},{1,25},{2,26},{3,27},{4,28},{5,29},{6,30},{7,31},{8,0},{9,1... | collective-permute-start | bytes 1572872 | tf_op jit(solution)/shard_map/ppermute | solution.py:127
  25.4 3.2 %collective-permute-start.9 = (bf16[256,1024]{1,0:T(8,128)(2,1)S(1)}, bf16[256,1024]{1,0:T(8,128)(2,1)}, u32[]{:S(2)}, u32[]{:S(2)}) collective-permute-start(bf16[256,1024]{1,0:T(8,128)(2,1)S(1)} %pad_maximum_fusion.1.refs_9_), channel_id=1, source_target_pairs={{0,2},{1,3},{2,4},{3,5},{4,6},{5,7},{6,0},{7,1},{8,10},{9,11},{10,... | collective-permute-start | bytes 1572872 | tf_op jit(solution)/shard_map/ppermute | solution.py:127
  28.9 7.2 %collective-permute-done.13.refs_14_ = bf16[256,1024]{1,0:T(8,128)(2,1)} collective-permute-done((bf16[256,1024]{1,0:T(8,128)(2,1)}, bf16[256,1024]{1,0:T(8,128)(2,1)}, u32[]{:S(2)}, u32[]{:S(2)}) %collective-permute-start.13) | collective-permute-done | bytes 524320 | tf_op jit(solution)/shard_map/ppermute | solution.py:127
  41.6 9.1 %collective-permute-done.15.refs_6_ = bf16[256,1024]{1,0:T(8,128)(2,1)S(1)} collective-permute-done((bf16[256,1024]{1,0:T(8,128)(2,1)}, bf16[256,1024]{1,0:T(8,128)(2,1)S(1)}, u32[]{:S(2)}, u32[]{:S(2)}) %collective-permute-start.15) | collective-permute-done | bytes 524320 | tf_op jit(solution)/shard_map/ppermute | solution.py:127
  52.6 3.1 %collective-permute-start.7 = (bf16[256,1024]{1,0:T(8,128)(2,1)}, bf16[256,1024]{1,0:T(8,128)(2,1)}, u32[]{:S(2)}, u32[]{:S(2)}) collective-permute-start(bf16[256,1024]{1,0:T(8,128)(2,1)} %collective-permute-done.6.refs_8_), channel_id=1, source_target_pairs={{0,24},{1,25},{2,26},{3,27},{4,28},{5,29},{6,30},{7,31},{8,0},{9,1... | collective-permute-start | bytes 1572872 | tf_op jit(solution)/shard_map/ppermute | solution.py:127
  60.6 7.4 %product_near.1 = (f32[16,2,128,128]{3,2,1,0:T(8,128)S(1)}, f32[2,128,128]{2,1,0:T(8,128)S(1)}) custom-call(s32[16]{0:T(128)S(1)} %stack.67.refs_0_.where, bf16[128,2048]{1,0:T(8,128)(2,1)S(1)} %copy-done.1, bf16[128,2048]{1,0:T(8,128)(2,1)S(1)} %copy-done.3, bf16[256,1024]{1,0:T(8,128)(2,1)S(1)} %pad_maximum_fusion.refs_3_, ...), custom_call_target="tpu_custom_call" | custom-call | tf_op jit(solution)/shard_map/product_near/pallas_call | solution.py:178
  68.1 3.1 %collective-permute-done.3.refs_3_ = bf16[256,1024]{1,0:T(8,128)(2,1)} collective-permute-done((bf16[256,1024]{1,0:T(8,128)(2,1)}, bf16[256,1024]{1,0:T(8,128)(2,1)}, u32[]{:S(2)}, u32[]{:S(2)}) %collective-permute-start.3) | collective-permute-done | bytes 524320 | tf_op jit(solution)/shard_map/ppermute | solution.py:127
  71.2 3.8 %product_far.1 = (f32[16,2,128,128]{3,2,1,0:T(8,128)S(1)}, f32[2,128,128]{2,1,0:T(8,128)S(1)}) custom-call(s32[16]{0:T(128)S(1)} %stack.67.refs_0_.where, bf16[128,2048]{1,0:T(8,128)(2,1)S(1)} %copy-done.1, bf16[128,2048]{1,0:T(8,128)(2,1)S(1)} %copy-done.3, bf16[256,1024]{1,0:T(8,128)(2,1)} %collective-permute-done.3.refs_3_, ...), custom_call_target="tpu_custom_call", output_to_operand_aliasing={{0}: (7, {})} | custom-call | tf_op jit(solution)/shard_map/product_far/pallas_call | solution.py:190
  76.4 2.4 %token_grads.1 = bf16[16,2,128,128]{3,2,1,0:T(8,128)(2,1)S(1)} custom-call(s32[16]{0:T(128)S(1)} %stack.67.refs_0_.where, f32[16,2,128,128]{3,2,1,0:T(8,128)S(1)} %get-tuple-element.12.ng, f32[2,128,128]{2,1,0:T(8,128)S(1)} %get-tuple-element.13.ss, f32[2,128,128]{2,1,0:T(8,128)S(1)} %get-tuple-element.14.inner, ...), custom_call_target="tpu_custom_call" | custom-call | tf_op jit(solution)/shard_map/token_grads/pallas_call | solution.py:199
  78.8 19.4 %all_to_all.14 = bf16[16,256,128]{2,1,0:T(8,128)(2,1)S(1)} all-to-all(bf16[16,256,128]{2,1,0:T(8,128)(2,1)S(1)} %bitcast.48), channel_id=1, replica_groups={{0,2,4,6,8,10,12,14,16,18,20,22,24,26,28,30},{1,3,5,7,9,11,13,15,17,19,..., dimensions={0} | all-to-all | bytes 2097152 | tf_op jit(solution)/shard_map/all_to_all | solution.py:356
  103.4 6.7 %all-to-all-start.1 = ((s32[128,1,384]{2,1,0:T(1,128)}), s32[128,1,384]{2,1,0:T(1,128)S(1)}, u32[]{:S(2)}, u32[]{:S(2)}) async-start(s32[128,1,384]{2,1,0:T(1,128)} %all_to_all.10), calls=%async_computation.1 | async-start | bytes 393216 | tf_op jit(solution)/shard_map/all_to_all | solution.py:334
  113.4 2.0 %collective-permute-start.23 = (bf16[16,128,128]{2,1,0:T(8,128)(2,1)S(1)}, bf16[16,128,128]{2,1,0:T(8,128)(2,1)S(1)}, u32[]{:S(2)}, u32[]{:S(2)}) collective-permute-start(bf16[16,128,128]{2,1,0:T(8,128)(2,1)S(1)} %collective-permute-done.22.refs_0_), channel_id=1, source_target_pairs={{0,32},{32,64},{64,96},{96,0},{1,33},{33,65},{65,97},{97,1},{2,34}... | collective-permute-start | bytes 1572872 | tf_op jit(solution)/shard_map/ppermute | solution.py:308
  115.3 3.0 %collective-permute-start.25 = (bf16[16,128,128]{2,1,0:T(8,128)(2,1)S(1)}, bf16[16,128,128]{2,1,0:T(8,128)(2,1)}, u32[]{:S(2)}, u32[]{:S(2)}) collective-permute-start(bf16[16,128,128]{2,1,0:T(8,128)(2,1)S(1)} %collective-permute-done.24.refs_1_), channel_id=1, source_target_pairs={{0,96},{32,0},{64,32},{96,64},{1,97},{33,1},{65,33},{97,65},{2,98}... | collective-permute-start | bytes 1572872 | tf_op jit(solution)/shard_map/ppermute | solution.py:308
  119.4 7.5 %scatter_rows.4.refs_3_ = f32[8200,128]{1,0:T(8,128)S(1)} custom-call(s32[4096]{0:T(1024)S(1)} %get-tuple-element.31.rows, s32[32]{0:T(128)S(1)} %get-tuple-element.30.counts, bf16[32,128,128]{2,1,0:T(8,128)(2,1)S(1)} %bitcast.47, s32[32,2,128]{2,1,0:T(2,128)S(1)} %reshape.174.refs_1_), custom_call_target="tpu_custom_call" | custom-call | flops 1000000 | bytes 28800000 | tf_op jit(solution)/shard_map/scatter_rows/pallas_call | solution.py:285
  127.1 8.1 %scatter_rows.5.refs_3_ = f32[8200,128]{1,0:T(8,128)S(1)} custom-call(s32[8192]{0:T(1024)S(1)} %get-tuple-element.29.rows, s32[64]{0:T(128)S(1)} %get-tuple-element.28.counts, bf16[16,128,128]{2,1,0:T(8,128)(2,1)S(1)} %collective-permute-done.22.refs_0_, bf16[16,128,128]{2,1,0:T(8,128)(2,1)S(1)} %collective-permute-done.24.refs_1_, ...), custom_call_target="tpu_custom_call", output_to_operand_aliasing={{}: (5, {})} | custom-call | flops 1000000 | bytes 28800000 | tf_op jit(solution)/shard_map/scatter_rows/pallas_call | solution.py:285
  135.3 9.3 %scatter_rows.6.refs_3_ = f32[8200,128]{1,0:T(8,128)S(1)} custom-call(s32[8192]{0:T(1024)S(1)} %get-tuple-element.29.rows, s32[64]{0:T(128)S(1)} %get-tuple-element.28.counts, bf16[16,128,128]{2,1,0:T(8,128)(2,1)} %collective-permute-done.26.refs_0_, bf16[16,128,128]{2,1,0:T(8,128)(2,1)} %collective-permute-done.27.refs_1_, ...), custom_call_target="tpu_custom_call", output_to_operand_aliasing={{}: (5, {})} | custom-call | flops 1000000 | bytes 28800000 | tf_op jit(solution)/shard_map/scatter_rows/pallas_call | solution.py:285
  144.6 8.9 %scatter_rows.7 = f32[8200,128]{1,0:T(8,128)S(1)} custom-call(s32[4096]{0:T(1024)S(1)} %get-tuple-element.33.rows, s32[32]{0:T(128)S(1)} %get-tuple-element.32.counts, bf16[16,128,128]{2,1,0:T(8,128)(2,1)S(1)} %collective-permute-done.23.refs_0_, bf16[16,128,128]{2,1,0:T(8,128)(2,1)} %collective-permute-done.25.refs_1_, ...), custom_call_target="tpu_custom_call", output_to_operand_aliasing={{}: (5, {})} | custom-call | flops 1000000 | bytes 28800000 | tf_op jit(solution)/shard_map/scatter_rows/pallas_call | solution.py:285
  155.9 4.3 %collective-permute-start.29 = (f32[64,128]{1,0:T(8,128)S(1)}, f32[64,128]{1,0:T(8,128)S(1)}, u32[]{:S(2)}, u32[]{:S(2)}) collective-permute-start(f32[64,128]{1,0:T(8,128)S(1)} %bitcast_add_fusion.1), channel_id=1, source_target_pairs={{0,4},{1,5},{2,6},{3,7},{4,0},{5,1},{6,2},{7,3},{8,12},{9,13},{10,... | collective-permute-start | bytes 98312 | tf_op jit(solution)/shard_map/ppermute | solution.py:127
  164.2 1.9 %collective-permute-done.31 = f32[64,128]{1,0:T(8,128)S(1)} collective-permute-done((f32[64,128]{1,0:T(8,128)S(1)}, f32[64,128]{1,0:T(8,128)S(1)}, u32[]{:S(2)}, u32[]{:S(2)}) %collective-permute-start.31) | collective-permute-done | bytes 32800 | tf_op jit(solution)/shard_map/ppermute | solution.py:127
  167.7 2.9 %collective-permute-start.34 = (f32[64,128]{1,0:T(8,128)S(1)}, f32[64,128]{1,0:T(8,128)S(1)}, u32[]{:S(2)}, u32[]{:S(2)}) collective-permute-start(f32[64,128]{1,0:T(8,128)S(1)} %add_add_fusion), channel_id=1, source_target_pairs={{0,24},{1,25},{2,26},{3,27},{4,28},{5,29},{6,30},{7,31},{8,0},{9,1... | collective-permute-start | bytes 98312 | tf_op jit(solution)/shard_map/ppermute | solution.py:127
  173.1 4.7 %multiply_subtract_fusion = f32[8192,128]{1,0:T(8,128)} fusion(f32[8192,128]{1,0:T(8,128)S(1)} %copy-done.7, f32[8200,128]{1,0:T(8,128)S(1)} %scatter_rows.7, f32[8192]{0:T(1024)S(1)} %get-tuple-element.16), kind=kLoop, calls=%fused_computation | loop fusion | flops 2097152 | bytes 12615680 | tf_op jit(solution)/shard_map/sub | solution.py:379
  (120 shorter events, 47.2 us)
Async XLA Ops:
  7.9 12.8 %collective-permute-start.5 = (bf16[128,1024]{1,0:T(8,128)(2,1)S(1)}, bf16[128,1024]{1,0:T(8,128)(2,1)S(1)}, u32[]{:S(2)}, u32[]{:S(2)}) collective-permute-start(bf16[128,1024]{1,0:T(8,128)(2,1)S(1)} %get-tuple-element.23), channel_id=1, source_target_pairs={{0,6},{1,7},{2,0},{3,1},{4,2},{5,3},{6,4},{7,5},{8,14},{9,15},{10,... | collective-permute-start | bytes 786440 | tf_op jit(solution)/shard_map/ppermute | solution.py:127
  7.9 13.5 %collective-permute-start.1 = (bf16[128,1024]{1,0:T(8,128)(2,1)S(1)}, bf16[128,1024]{1,0:T(8,128)(2,1)}, u32[]{:S(2)}, u32[]{:S(2)}) collective-permute-start(bf16[128,1024]{1,0:T(8,128)(2,1)S(1)} %get-tuple-element.23), channel_id=1, source_target_pairs={{0,2},{1,3},{2,4},{3,5},{4,6},{5,7},{6,0},{7,1},{8,10},{9,11},{10,... | collective-permute-start | bytes 786440 | tf_op jit(solution)/shard_map/ppermute | solution.py:127
  12.1 12.4 %collective-permute-start.8 = (bf16[128,1024]{1,0:T(8,128)(2,1)S(1)}, bf16[128,1024]{1,0:T(8,128)(2,1)S(1)}, u32[]{:S(2)}, u32[]{:S(2)}) collective-permute-start(bf16[128,1024]{1,0:T(8,128)(2,1)S(1)} %get-tuple-element.22), channel_id=1, source_target_pairs={{0,8},{1,9},{2,10},{3,11},{4,12},{5,13},{6,14},{7,15},{8,16},{9,17... | collective-permute-start | bytes 786440 | tf_op jit(solution)/shard_map/ppermute | solution.py:127
  18.5 38.6 %collective-permute-start.19 = (bf16[128,4096]{1,0:T(8,128)(2,1)}, bf16[128,4096]{1,0:T(8,128)(2,1)S(1)}, u32[]{:S(2)}, u32[]{:S(2)}) collective-permute-start(bf16[128,4096]{1,0:T(8,128)(2,1)} %v_own.1), channel_id=1, source_target_pairs={{0,1},{1,0},{2,3},{3,2},{4,5},{5,4},{6,7},{7,6},{8,9},{9,8},{10,11... | collective-permute-start | bytes 3145736 | tf_op jit(solution)/shard_map/ppermute | solution.py:127
  20.7 15.4 %collective-permute-start.13 = (bf16[256,1024]{1,0:T(8,128)(2,1)}, bf16[256,1024]{1,0:T(8,128)(2,1)}, u32[]{:S(2)}, u32[]{:S(2)}) collective-permute-start(bf16[256,1024]{1,0:T(8,128)(2,1)} %constant_dynamic-update-slice_fusion.2.refs_10_), channel_id=1, source_target_pairs={{0,6},{1,7},{2,0},{3,1},{4,2},{5,3},{6,4},{7,5},{8,14},{9,15},{10,... | collective-permute-start | bytes 1572872 | tf_op jit(solution)/shard_map/ppermute | solution.py:127
  21.4 15.8 %collective-permute-start.6 = (bf16[256,1024]{1,0:T(8,128)(2,1)}, bf16[256,1024]{1,0:T(8,128)(2,1)}, u32[]{:S(2)}, u32[]{:S(2)}) collective-permute-start(bf16[256,1024]{1,0:T(8,128)(2,1)} %constant_dynamic-update-slice_fusion.refs_4_), channel_id=1, source_target_pairs={{0,24},{1,25},{2,26},{3,27},{4,28},{5,29},{6,30},{7,31},{8,0},{9,1... | collective-permute-start | bytes 1572872 | tf_op jit(solution)/shard_map/ppermute | solution.py:127
  24.5 15.4 %collective-permute-start.2 = (bf16[256,1024]{1,0:T(8,128)(2,1)S(1)}, bf16[256,1024]{1,0:T(8,128)(2,1)}, u32[]{:S(2)}, u32[]{:S(2)}) collective-permute-start(bf16[256,1024]{1,0:T(8,128)(2,1)S(1)} %pad_maximum_fusion.refs_3_), channel_id=1, source_target_pairs={{0,8},{1,9},{2,10},{3,11},{4,12},{5,13},{6,14},{7,15},{8,16},{9,17... | collective-permute-start | bytes 1572872 | tf_op jit(solution)/shard_map/ppermute | solution.py:127
  25.4 16.1 %collective-permute-start.9 = (bf16[256,1024]{1,0:T(8,128)(2,1)S(1)}, bf16[256,1024]{1,0:T(8,128)(2,1)}, u32[]{:S(2)}, u32[]{:S(2)}) collective-permute-start(bf16[256,1024]{1,0:T(8,128)(2,1)S(1)} %pad_maximum_fusion.1.refs_9_), channel_id=1, source_target_pairs={{0,2},{1,3},{2,4},{3,5},{4,6},{5,7},{6,0},{7,1},{8,10},{9,11},{10,... | collective-permute-start | bytes 1572872 | tf_op jit(solution)/shard_map/ppermute | solution.py:127
  36.0 14.7 %collective-permute-start.15 = (bf16[256,1024]{1,0:T(8,128)(2,1)}, bf16[256,1024]{1,0:T(8,128)(2,1)S(1)}, u32[]{:S(2)}, u32[]{:S(2)}) collective-permute-start(bf16[256,1024]{1,0:T(8,128)(2,1)} %constant_dynamic-update-slice_fusion.refs_4_), channel_id=1, source_target_pairs={{0,8},{1,9},{2,10},{3,11},{4,12},{5,13},{6,14},{7,15},{8,16},{9,17... | collective-permute-start | bytes 1572872 | tf_op jit(solution)/shard_map/ppermute | solution.py:127
  37.3 14.7 %collective-permute-start.17 = (bf16[256,1024]{1,0:T(8,128)(2,1)}, bf16[256,1024]{1,0:T(8,128)(2,1)}, u32[]{:S(2)}, u32[]{:S(2)}) collective-permute-start(bf16[256,1024]{1,0:T(8,128)(2,1)} %constant_dynamic-update-slice_fusion.2.refs_10_), channel_id=1, source_target_pairs={{0,2},{1,3},{2,4},{3,5},{4,6},{5,7},{6,0},{7,1},{8,10},{9,11},{10,... | collective-permute-start | bytes 1572872 | tf_op jit(solution)/shard_map/ppermute | solution.py:127
  39.8 12.8 %collective-permute-start.16 = (bf16[256,1024]{1,0:T(8,128)(2,1)S(1)}, bf16[256,1024]{1,0:T(8,128)(2,1)}, u32[]{:S(2)}, u32[]{:S(2)}) collective-permute-start(bf16[256,1024]{1,0:T(8,128)(2,1)S(1)} %pad_maximum_fusion.refs_3_), channel_id=1, source_target_pairs={{0,24},{1,25},{2,26},{3,27},{4,28},{5,29},{6,30},{7,31},{8,0},{9,1... | collective-permute-start | bytes 1572872 | tf_op jit(solution)/shard_map/ppermute | solution.py:127
  41.4 14.3 %collective-permute-start.18 = (bf16[256,1024]{1,0:T(8,128)(2,1)S(1)}, bf16[256,1024]{1,0:T(8,128)(2,1)}, u32[]{:S(2)}, u32[]{:S(2)}) collective-permute-start(bf16[256,1024]{1,0:T(8,128)(2,1)S(1)} %pad_maximum_fusion.1.refs_9_), channel_id=1, source_target_pairs={{0,6},{1,7},{2,0},{3,1},{4,2},{5,3},{6,4},{7,5},{8,14},{9,15},{10,... | collective-permute-start | bytes 1572872 | tf_op jit(solution)/shard_map/ppermute | solution.py:127
  51.5 23.5 %collective-permute-start.21 = (bf16[128,4096]{1,0:T(8,128)(2,1)}, bf16[128,4096]{1,0:T(8,128)(2,1)}, u32[]{:S(2)}, u32[]{:S(2)}) collective-permute-start(bf16[128,4096]{1,0:T(8,128)(2,1)} %r_own.1), channel_id=1, source_target_pairs={{0,1},{1,0},{2,3},{3,2},{4,5},{5,4},{6,7},{7,6},{8,9},{9,8},{10,11... | collective-permute-start | bytes 3145736 | tf_op jit(solution)/shard_map/ppermute | solution.py:127
  52.0 16.0 %collective-permute-start.14 = (bf16[256,1024]{1,0:T(8,128)(2,1)}, bf16[256,1024]{1,0:T(8,128)(2,1)}, u32[]{:S(2)}, u32[]{:S(2)}) collective-permute-start(bf16[256,1024]{1,0:T(8,128)(2,1)} %collective-permute-done.13.refs_14_), channel_id=1, source_target_pairs={{0,6},{1,7},{2,0},{3,1},{4,2},{5,3},{6,4},{7,5},{8,14},{9,15},{10,... | collective-permute-start | bytes 1572872 | tf_op jit(solution)/shard_map/ppermute | solution.py:127
  52.6 15.4 %collective-permute-start.7 = (bf16[256,1024]{1,0:T(8,128)(2,1)}, bf16[256,1024]{1,0:T(8,128)(2,1)}, u32[]{:S(2)}, u32[]{:S(2)}) collective-permute-start(bf16[256,1024]{1,0:T(8,128)(2,1)} %collective-permute-done.6.refs_8_), channel_id=1, source_target_pairs={{0,24},{1,25},{2,26},{3,27},{4,28},{5,29},{6,30},{7,31},{8,0},{9,1... | collective-permute-start | bytes 1572872 | tf_op jit(solution)/shard_map/ppermute | solution.py:127
  55.7 12.4 %collective-permute-start.10 = (bf16[256,1024]{1,0:T(8,128)(2,1)}, bf16[256,1024]{1,0:T(8,128)(2,1)}, u32[]{:S(2)}, u32[]{:S(2)}) collective-permute-start(bf16[256,1024]{1,0:T(8,128)(2,1)} %collective-permute-done.9.refs_11_), channel_id=1, source_target_pairs={{0,2},{1,3},{2,4},{3,5},{4,6},{5,7},{6,0},{7,1},{8,10},{9,11},{10,... | collective-permute-start | bytes 1572872 | tf_op jit(solution)/shard_map/ppermute | solution.py:127
  57.1 14.1 %collective-permute-start.3 = (bf16[256,1024]{1,0:T(8,128)(2,1)}, bf16[256,1024]{1,0:T(8,128)(2,1)}, u32[]{:S(2)}, u32[]{:S(2)}) collective-permute-start(bf16[256,1024]{1,0:T(8,128)(2,1)} %collective-permute-done.2.refs_5_), channel_id=1, source_target_pairs={{0,8},{1,9},{2,10},{3,11},{4,12},{5,13},{6,14},{7,15},{8,16},{9,17... | collective-permute-start | bytes 1572872 | tf_op jit(solution)/shard_map/ppermute | solution.py:127
  99.2 14.1 %collective-permute-start.22 = (bf16[16,128,128]{2,1,0:T(8,128)(2,1)}, bf16[16,128,128]{2,1,0:T(8,128)(2,1)S(1)}, u32[]{:S(2)}, u32[]{:S(2)}) collective-permute-start(bf16[16,128,128]{2,1,0:T(8,128)(2,1)} %bitcast.20), channel_id=1, source_target_pairs={{0,32},{32,64},{64,96},{96,0},{1,33},{33,65},{65,97},{97,1},{2,34}... | collective-permute-start | bytes 1572872 | tf_op jit(solution)/shard_map/ppermute | solution.py:308
  100.8 14.5 %collective-permute-start.24 = (bf16[16,128,128]{2,1,0:T(8,128)(2,1)}, bf16[16,128,128]{2,1,0:T(8,128)(2,1)S(1)}, u32[]{:S(2)}, u32[]{:S(2)}) collective-permute-start(bf16[16,128,128]{2,1,0:T(8,128)(2,1)} %bitcast.21), channel_id=1, source_target_pairs={{0,96},{32,0},{64,32},{96,64},{1,97},{33,1},{65,33},{97,65},{2,98}... | collective-permute-start | bytes 1572872 | tf_op jit(solution)/shard_map/ppermute | solution.py:308
  103.4 15.7 %all-to-all-start.1 = ((s32[128,1,384]{2,1,0:T(1,128)}), s32[128,1,384]{2,1,0:T(1,128)S(1)}, u32[]{:S(2)}, u32[]{:S(2)}) async-start(s32[128,1,384]{2,1,0:T(1,128)} %all_to_all.10), calls=%async_computation.1 | async-start | bytes 393216 | tf_op jit(solution)/shard_map/all_to_all | solution.py:334
  110.0 25.2 %collective-permute-start.26 = (bf16[16,128,128]{2,1,0:T(8,128)(2,1)}, bf16[16,128,128]{2,1,0:T(8,128)(2,1)}, u32[]{:S(2)}, u32[]{:S(2)}) collective-permute-start(bf16[16,128,128]{2,1,0:T(8,128)(2,1)} %bitcast.21), channel_id=1, source_target_pairs={{0,32},{32,64},{64,96},{96,0},{1,33},{33,65},{65,97},{97,1},{2,34}... | collective-permute-start | bytes 1572872 | tf_op jit(solution)/shard_map/ppermute | solution.py:308
  111.6 23.7 %collective-permute-start.27 = (bf16[16,128,128]{2,1,0:T(8,128)(2,1)}, bf16[16,128,128]{2,1,0:T(8,128)(2,1)}, u32[]{:S(2)}, u32[]{:S(2)}) collective-permute-start(bf16[16,128,128]{2,1,0:T(8,128)(2,1)} %bitcast.20), channel_id=1, source_target_pairs={{0,96},{32,0},{64,32},{96,64},{1,97},{33,1},{65,33},{97,65},{2,98}... | collective-permute-start | bytes 1572872 | tf_op jit(solution)/shard_map/ppermute | solution.py:308
  113.4 31.2 %collective-permute-start.23 = (bf16[16,128,128]{2,1,0:T(8,128)(2,1)S(1)}, bf16[16,128,128]{2,1,0:T(8,128)(2,1)S(1)}, u32[]{:S(2)}, u32[]{:S(2)}) collective-permute-start(bf16[16,128,128]{2,1,0:T(8,128)(2,1)S(1)} %collective-permute-done.22.refs_0_), channel_id=1, source_target_pairs={{0,32},{32,64},{64,96},{96,0},{1,33},{33,65},{65,97},{97,1},{2,34}... | collective-permute-start | bytes 1572872 | tf_op jit(solution)/shard_map/ppermute | solution.py:308
  115.3 29.2 %collective-permute-start.25 = (bf16[16,128,128]{2,1,0:T(8,128)(2,1)S(1)}, bf16[16,128,128]{2,1,0:T(8,128)(2,1)}, u32[]{:S(2)}, u32[]{:S(2)}) collective-permute-start(bf16[16,128,128]{2,1,0:T(8,128)(2,1)S(1)} %collective-permute-done.24.refs_1_), channel_id=1, source_target_pairs={{0,96},{32,0},{64,32},{96,64},{1,97},{33,1},{65,33},{97,65},{2,98}... | collective-permute-start | bytes 1572872 | tf_op jit(solution)/shard_map/ppermute | solution.py:308
  (23 other events, 290.6 us)
where the time goes:
time: 178 us
  starting transfers between devices  55.8 us (31%)
  Pallas kernels  47.3 us (27%)
  waiting for transfers between devices  33.5 us (19%)
  blocking collectives  19.4 us (11%)
  local copies, waits for them, and re-layouts  12.2 us (7%)
  other arithmetic  8.41 us (5%)
    ppermute x29, starting transfers between devices, shifted(): return lax.ppermute(value, 'col', pairs)  37.7 us
    pallas_call x4, Pallas kernels, scattered(): pl.pallas_call(functools.partial(scatter_kernel, held is None, parts, ind...  33.8 us
    ppermute x29, waiting for transfers between devices, shifted(): return lax.ppermute(value, 'col', pairs)  32.7 us
    all_to_all x1, blocking collectives, shards(): lax.all_to_all(grads.reshape(columns // 2, 2 * tok, lanes), 'col', 0, 0,...  19.4 us
    ppermute x6, starting transfers between devices, ring(): return lax.ppermute(x, 'group', [(d, (d + by) % n) for d in range(n)])  11.5 us
    pallas_call x1, Pallas kernels, token_grads(): vmem_call(functools.partial(product_kernel, pieces, True, False, columns)...  7.38 us
    unnamed x26, local copies, waits for them, and re-layouts  7.01 us
    all_to_all x1, starting transfers between devices, exchange(): lax.all_to_all(sent.reshape(groups * columns, -1), ('group', 'col'), 0, 0...  6.67 us
  transfers between devices with their start and end apart: 36, of which 14 were waited for; matrix products, arithmetic and copies ran while one was open for 4% of the time, Pallas kernels for 20%

commit v1 on v0

--- a/solution.py
+++ b/solution.py
@@ -259,7 +259,7 @@
 
         return carry
 
-    lax.fori_loop(0, per, block, 0)
+    lax.fori_loop(0, per, block, 0, unroll=2)
 
 
 def scattered(xs, maps, rows, counts, held, skips=(0, 0)):

time: 178 us -> 176 us (0.989)
  the two profiles are of different devices: /device:TPU:6 before, /device:TPU:22 now
where the time goes in v1:
time: 176 us
  starting transfers between devices  52.2 us (30%)
  Pallas kernels  46.8 us (27%)
  waiting for transfers between devices  35.7 us (20%)
  blocking collectives  19.4 us (11%)
  local copies, waits for them, and re-layouts  12.2 us (7%)
  other arithmetic  8.41 us (5%)
    ppermute x29, starting transfers between devices, shifted(): return lax.ppermute(value, 'col', pairs)  38.4 us
    pallas_call x4, Pallas kernels, scattered(): pl.pallas_call(functools.partial(scatter_kernel, held is None, parts, ind...  33.3 us
    ppermute x29, waiting for transfers between devices, shifted(): return lax.ppermute(value, 'col', pairs)  32.7 us
    all_to_all x1, blocking collectives, shards(): lax.all_to_all(grads.reshape(columns // 2, 2 * tok, lanes), 'col', 0, 0,...  19.4 us
    all_to_all x1, starting transfers between devices, exchange(): lax.all_to_all(sent.reshape(groups * columns, -1), ('group', 'col'), 0, 0...  7.69 us
    pallas_call x1, Pallas kernels, token_grads(): vmem_call(functools.partial(product_kernel, pieces, True, False, columns)...  7.39 us
    unnamed x26, local copies, waits for them, and re-layouts  7.01 us
    ppermute x6, starting transfers between devices, ring(): return lax.ppermute(x, 'group', [(d, (d + by) % n) for d in range(n)])  6.15 us
  transfers between devices with their start and end apart: 36, of which 14 were waited for; matrix products, arithmetic and copies ran while one was open for 4% of the time, Pallas kernels for 20%

profile of v1, /device:TPU:22, one launch (start us, length us, event | category | flops | bytes accessed | tf_op | source)
XLA Modules:
  0.0 175.9 jit_solution(248905476462140685)
XLA Ops:
  1.8 4.0 %collective-permute-start.11 = (bf16[128,1024]{1,0:T(8,128)(2,1)S(1)}, bf16[128,1024]{1,0:T(8,128)(2,1)S(1)}, u32[]{:S(2)}, u32[]{:S(2)}) collective-permute-start(bf16[128,1024]{1,0:T(8,128)(2,1)S(1)} %get-tuple-element.22), channel_id=1, source_target_pairs={{0,16},{1,17},{2,18},{3,19},{4,20},{5,21},{6,22},{7,23},{8,24},{9,... | collective-permute-start | bytes 786440 | tf_op jit(solution)/shard_map/ppermute | solution.py:127
  7.9 3.2 %collective-permute-start.1 = (bf16[128,1024]{1,0:T(8,128)(2,1)S(1)}, bf16[128,1024]{1,0:T(8,128)(2,1)}, u32[]{:S(2)}, u32[]{:S(2)}) collective-permute-start(bf16[128,1024]{1,0:T(8,128)(2,1)S(1)} %get-tuple-element.23), channel_id=1, source_target_pairs={{0,2},{1,3},{2,4},{3,5},{4,6},{5,7},{6,0},{7,1},{8,10},{9,11},{10,... | collective-permute-start | bytes 786440 | tf_op jit(solution)/shard_map/ppermute | solution.py:127
  12.1 2.5 %collective-permute-start.8 = (bf16[128,1024]{1,0:T(8,128)(2,1)S(1)}, bf16[128,1024]{1,0:T(8,128)(2,1)S(1)}, u32[]{:S(2)}, u32[]{:S(2)}) collective-permute-start(bf16[128,1024]{1,0:T(8,128)(2,1)S(1)} %get-tuple-element.22), channel_id=1, source_target_pairs={{0,8},{1,9},{2,10},{3,11},{4,12},{5,13},{6,14},{7,15},{8,16},{9,17... | collective-permute-start | bytes 786440 | tf_op jit(solution)/shard_map/ppermute | solution.py:127
  21.4 2.0 %collective-permute-start.6 = (bf16[256,1024]{1,0:T(8,128)(2,1)}, bf16[256,1024]{1,0:T(8,128)(2,1)}, u32[]{:S(2)}, u32[]{:S(2)}) collective-permute-start(bf16[256,1024]{1,0:T(8,128)(2,1)} %constant_dynamic-update-slice_fusion.refs_4_), channel_id=1, source_target_pairs={{0,24},{1,25},{2,26},{3,27},{4,28},{5,29},{6,30},{7,31},{8,0},{9,1... | collective-permute-start | bytes 1572872 | tf_op jit(solution)/shard_map/ppermute | solution.py:127
  25.4 3.2 %collective-permute-start.9 = (bf16[256,1024]{1,0:T(8,128)(2,1)S(1)}, bf16[256,1024]{1,0:T(8,128)(2,1)}, u32[]{:S(2)}, u32[]{:S(2)}) collective-permute-start(bf16[256,1024]{1,0:T(8,128)(2,1)S(1)} %pad_maximum_fusion.1.refs_9_), channel_id=1, source_target_pairs={{0,2},{1,3},{2,4},{3,5},{4,6},{5,7},{6,0},{7,1},{8,10},{9,11},{10,... | collective-permute-start | bytes 1572872 | tf_op jit(solution)/shard_map/ppermute | solution.py:127
  28.9 7.2 %collective-permute-done.13.refs_14_ = bf16[256,1024]{1,0:T(8,128)(2,1)} collective-permute-done((bf16[256,1024]{1,0:T(8,128)(2,1)}, bf16[256,1024]{1,0:T(8,128)(2,1)}, u32[]{:S(2)}, u32[]{:S(2)}) %collective-permute-start.13) | collective-permute-done | bytes 524320 | tf_op jit(solution)/shard_map/ppermute | solution.py:127
  41.6 9.1 %collective-permute-done.15.refs_6_ = bf16[256,1024]{1,0:T(8,128)(2,1)S(1)} collective-permute-done((bf16[256,1024]{1,0:T(8,128)(2,1)}, bf16[256,1024]{1,0:T(8,128)(2,1)S(1)}, u32[]{:S(2)}, u32[]{:S(2)}) %collective-permute-start.15) | collective-permute-done | bytes 524320 | tf_op jit(solution)/shard_map/ppermute | solution.py:127
  52.6 3.1 %collective-permute-start.7 = (bf16[256,1024]{1,0:T(8,128)(2,1)}, bf16[256,1024]{1,0:T(8,128)(2,1)}, u32[]{:S(2)}, u32[]{:S(2)}) collective-permute-start(bf16[256,1024]{1,0:T(8,128)(2,1)} %collective-permute-done.6.refs_8_), channel_id=1, source_target_pairs={{0,24},{1,25},{2,26},{3,27},{4,28},{5,29},{6,30},{7,31},{8,0},{9,1... | collective-permute-start | bytes 1572872 | tf_op jit(solution)/shard_map/ppermute | solution.py:127
  60.6 7.4 %product_near.1 = (f32[16,2,128,128]{3,2,1,0:T(8,128)S(1)}, f32[2,128,128]{2,1,0:T(8,128)S(1)}) custom-call(s32[16]{0:T(128)S(1)} %stack.67.refs_0_.where, bf16[128,2048]{1,0:T(8,128)(2,1)S(1)} %copy-done.1, bf16[128,2048]{1,0:T(8,128)(2,1)S(1)} %copy-done.3, bf16[256,1024]{1,0:T(8,128)(2,1)S(1)} %pad_maximum_fusion.refs_3_, ...), custom_call_target="tpu_custom_call" | custom-call | tf_op jit(solution)/shard_map/product_near/pallas_call | solution.py:178
  68.1 3.1 %collective-permute-done.3.refs_3_ = bf16[256,1024]{1,0:T(8,128)(2,1)} collective-permute-done((bf16[256,1024]{1,0:T(8,128)(2,1)}, bf16[256,1024]{1,0:T(8,128)(2,1)}, u32[]{:S(2)}, u32[]{:S(2)}) %collective-permute-start.3) | collective-permute-done | bytes 524320 | tf_op jit(solution)/shard_map/ppermute | solution.py:127
  71.2 3.8 %product_far.1 = (f32[16,2,128,128]{3,2,1,0:T(8,128)S(1)}, f32[2,128,128]{2,1,0:T(8,128)S(1)}) custom-call(s32[16]{0:T(128)S(1)} %stack.67.refs_0_.where, bf16[128,2048]{1,0:T(8,128)(2,1)S(1)} %copy-done.1, bf16[128,2048]{1,0:T(8,128)(2,1)S(1)} %copy-done.3, bf16[256,1024]{1,0:T(8,128)(2,1)} %collective-permute-done.3.refs_3_, ...), custom_call_target="tpu_custom_call", output_to_operand_aliasing={{0}: (7, {})} | custom-call | tf_op jit(solution)/shard_map/product_far/pallas_call | solution.py:190
  76.4 2.4 %token_grads.1 = bf16[16,2,128,128]{3,2,1,0:T(8,128)(2,1)S(1)} custom-call(s32[16]{0:T(128)S(1)} %stack.67.refs_0_.where, f32[16,2,128,128]{3,2,1,0:T(8,128)S(1)} %get-tuple-element.12.ng, f32[2,128,128]{2,1,0:T(8,128)S(1)} %get-tuple-element.13.ss, f32[2,128,128]{2,1,0:T(8,128)S(1)} %get-tuple-element.14.inner, ...), custom_call_target="tpu_custom_call" | custom-call | tf_op jit(solution)/shard_map/token_grads/pallas_call | solution.py:199
  78.8 19.4 %all_to_all.14 = bf16[16,256,128]{2,1,0:T(8,128)(2,1)S(1)} all-to-all(bf16[16,256,128]{2,1,0:T(8,128)(2,1)S(1)} %bitcast.48), channel_id=1, replica_groups={{0,2,4,6,8,10,12,14,16,18,20,22,24,26,28,30},{1,3,5,7,9,11,13,15,17,19,..., dimensions={0} | all-to-all | bytes 2097152 | tf_op jit(solution)/shard_map/all_to_all | solution.py:356
  102.2 7.7 %all-to-all-start.1 = ((s32[128,1,384]{2,1,0:T(1,128)}), s32[128,1,384]{2,1,0:T(1,128)S(1)}, u32[]{:S(2)}, u32[]{:S(2)}) async-start(s32[128,1,384]{2,1,0:T(1,128)} %all_to_all.10), calls=%async_computation.1 | async-start | bytes 393216 | tf_op jit(solution)/shard_map/all_to_all | solution.py:334
  112.0 2.0 %collective-permute-done.22.refs_0_ = bf16[16,128,128]{2,1,0:T(8,128)(2,1)S(1)} collective-permute-done((bf16[16,128,128]{2,1,0:T(8,128)(2,1)}, bf16[16,128,128]{2,1,0:T(8,128)(2,1)S(1)}, u32[]{:S(2)}, u32[]{:S(2)}) %collective-permute-start.22) | collective-permute-done | bytes 524320 | tf_op jit(solution)/shard_map/ppermute | solution.py:308
  117.3 7.4 %scatter_rows.4.refs_3_ = f32[8200,128]{1,0:T(8,128)S(1)} custom-call(s32[4096]{0:T(1024)S(1)} %get-tuple-element.31.rows, s32[32]{0:T(128)S(1)} %get-tuple-element.30.counts, bf16[32,128,128]{2,1,0:T(8,128)(2,1)S(1)} %bitcast.47, s32[32,2,128]{2,1,0:T(2,128)S(1)} %reshape.174.refs_1_), custom_call_target="tpu_custom_call" | custom-call | flops 1000000 | bytes 28800000 | tf_op jit(solution)/shard_map/scatter_rows/pallas_call | solution.py:285
  124.9 8.0 %scatter_rows.5.refs_3_ = f32[8200,128]{1,0:T(8,128)S(1)} custom-call(s32[8192]{0:T(1024)S(1)} %get-tuple-element.29.rows, s32[64]{0:T(128)S(1)} %get-tuple-element.28.counts, bf16[16,128,128]{2,1,0:T(8,128)(2,1)S(1)} %collective-permute-done.22.refs_0_, bf16[16,128,128]{2,1,0:T(8,128)(2,1)S(1)} %collective-permute-done.24.refs_1_, ...), custom_call_target="tpu_custom_call", output_to_operand_aliasing={{}: (5, {})} | custom-call | flops 1000000 | bytes 28800000 | tf_op jit(solution)/shard_map/scatter_rows/pallas_call | solution.py:285
  132.9 9.2 %scatter_rows.6.refs_3_ = f32[8200,128]{1,0:T(8,128)S(1)} custom-call(s32[8192]{0:T(1024)S(1)} %get-tuple-element.29.rows, s32[64]{0:T(128)S(1)} %get-tuple-element.28.counts, bf16[16,128,128]{2,1,0:T(8,128)(2,1)} %collective-permute-done.26.refs_0_, bf16[16,128,128]{2,1,0:T(8,128)(2,1)} %collective-permute-done.27.refs_1_, ...), custom_call_target="tpu_custom_call", output_to_operand_aliasing={{}: (5, {})} | custom-call | flops 1000000 | bytes 28800000 | tf_op jit(solution)/shard_map/scatter_rows/pallas_call | solution.py:285
  142.1 8.7 %scatter_rows.7 = f32[8200,128]{1,0:T(8,128)S(1)} custom-call(s32[4096]{0:T(1024)S(1)} %get-tuple-element.33.rows, s32[32]{0:T(128)S(1)} %get-tuple-element.32.counts, bf16[16,128,128]{2,1,0:T(8,128)(2,1)S(1)} %collective-permute-done.23.refs_0_, bf16[16,128,128]{2,1,0:T(8,128)(2,1)} %collective-permute-done.25.refs_1_, ...), custom_call_target="tpu_custom_call", output_to_operand_aliasing={{}: (5, {})} | custom-call | flops 1000000 | bytes 28800000 | tf_op jit(solution)/shard_map/scatter_rows/pallas_call | solution.py:285
  153.3 3.9 %collective-permute-start.29 = (f32[64,128]{1,0:T(8,128)S(1)}, f32[64,128]{1,0:T(8,128)S(1)}, u32[]{:S(2)}, u32[]{:S(2)}) collective-permute-start(f32[64,128]{1,0:T(8,128)S(1)} %bitcast_add_fusion.1), channel_id=1, source_target_pairs={{0,4},{1,5},{2,6},{3,7},{4,0},{5,1},{6,2},{7,3},{8,12},{9,13},{10,... | collective-permute-start | bytes 98312 | tf_op jit(solution)/shard_map/ppermute | solution.py:127
  159.3 1.9 %collective-permute-done.30 = f32[64,128]{1,0:T(8,128)S(1)} collective-permute-done((f32[64,128]{1,0:T(8,128)S(1)}, f32[64,128]{1,0:T(8,128)S(1)}, u32[]{:S(2)}, u32[]{:S(2)}) %collective-permute-start.30) | collective-permute-done | bytes 32800 | tf_op jit(solution)/shard_map/ppermute | solution.py:127
  163.0 2.4 %collective-permute-start.32 = (f32[64,128]{1,0:T(8,128)S(1)}, f32[64,128]{1,0:T(8,128)S(1)}, u32[]{:S(2)}, u32[]{:S(2)}) collective-permute-start(f32[64,128]{1,0:T(8,128)S(1)} %add_add_fusion), channel_id=1, source_target_pairs={{0,16},{1,17},{2,18},{3,19},{4,20},{5,21},{6,22},{7,23},{8,24},{9,... | collective-permute-start | bytes 98312 | tf_op jit(solution)/shard_map/ppermute | solution.py:127
  165.8 2.9 %collective-permute-start.34 = (f32[64,128]{1,0:T(8,128)S(1)}, f32[64,128]{1,0:T(8,128)S(1)}, u32[]{:S(2)}, u32[]{:S(2)}) collective-permute-start(f32[64,128]{1,0:T(8,128)S(1)} %add_add_fusion), channel_id=1, source_target_pairs={{0,24},{1,25},{2,26},{3,27},{4,28},{5,29},{6,30},{7,31},{8,0},{9,1... | collective-permute-start | bytes 98312 | tf_op jit(solution)/shard_map/ppermute | solution.py:127
  171.2 4.7 %multiply_subtract_fusion = f32[8192,128]{1,0:T(8,128)} fusion(f32[8192,128]{1,0:T(8,128)S(1)} %copy-done.7, f32[8200,128]{1,0:T(8,128)S(1)} %scatter_rows.7, f32[8192]{0:T(1024)S(1)} %get-tuple-element.16), kind=kLoop, calls=%fused_computation | loop fusion | flops 2097152 | bytes 12615680 | tf_op jit(solution)/shard_map/sub | solution.py:379
  (120 shorter events, 45.7 us)
Async XLA Ops:
  7.9 12.8 %collective-permute-start.5 = (bf16[128,1024]{1,0:T(8,128)(2,1)S(1)}, bf16[128,1024]{1,0:T(8,128)(2,1)S(1)}, u32[]{:S(2)}, u32[]{:S(2)}) collective-permute-start(bf16[128,1024]{1,0:T(8,128)(2,1)S(1)} %get-tuple-element.23), channel_id=1, source_target_pairs={{0,6},{1,7},{2,0},{3,1},{4,2},{5,3},{6,4},{7,5},{8,14},{9,15},{10,... | collective-permute-start | bytes 786440 | tf_op jit(solution)/shard_map/ppermute | solution.py:127
  7.9 13.5 %collective-permute-start.1 = (bf16[128,1024]{1,0:T(8,128)(2,1)S(1)}, bf16[128,1024]{1,0:T(8,128)(2,1)}, u32[]{:S(2)}, u32[]{:S(2)}) collective-permute-start(bf16[128,1024]{1,0:T(8,128)(2,1)S(1)} %get-tuple-element.23), channel_id=1, source_target_pairs={{0,2},{1,3},{2,4},{3,5},{4,6},{5,7},{6,0},{7,1},{8,10},{9,11},{10,... | collective-permute-start | bytes 786440 | tf_op jit(solution)/shard_map/ppermute | solution.py:127
  12.1 12.4 %collective-permute-start.8 = (bf16[128,1024]{1,0:T(8,128)(2,1)S(1)}, bf16[128,1024]{1,0:T(8,128)(2,1)S(1)}, u32[]{:S(2)}, u32[]{:S(2)}) collective-permute-start(bf16[128,1024]{1,0:T(8,128)(2,1)S(1)} %get-tuple-element.22), channel_id=1, source_target_pairs={{0,8},{1,9},{2,10},{3,11},{4,12},{5,13},{6,14},{7,15},{8,16},{9,17... | collective-permute-start | bytes 786440 | tf_op jit(solution)/shard_map/ppermute | solution.py:127
  18.5 38.6 %collective-permute-start.19 = (bf16[128,4096]{1,0:T(8,128)(2,1)}, bf16[128,4096]{1,0:T(8,128)(2,1)S(1)}, u32[]{:S(2)}, u32[]{:S(2)}) collective-permute-start(bf16[128,4096]{1,0:T(8,128)(2,1)} %v_own.1), channel_id=1, source_target_pairs={{0,1},{1,0},{2,3},{3,2},{4,5},{5,4},{6,7},{7,6},{8,9},{9,8},{10,11... | collective-permute-start | bytes 3145736 | tf_op jit(solution)/shard_map/ppermute | solution.py:127
  20.7 15.4 %collective-permute-start.13 = (bf16[256,1024]{1,0:T(8,128)(2,1)}, bf16[256,1024]{1,0:T(8,128)(2,1)}, u32[]{:S(2)}, u32[]{:S(2)}) collective-permute-start(bf16[256,1024]{1,0:T(8,128)(2,1)} %constant_dynamic-update-slice_fusion.2.refs_10_), channel_id=1, source_target_pairs={{0,6},{1,7},{2,0},{3,1},{4,2},{5,3},{6,4},{7,5},{8,14},{9,15},{10,... | collective-permute-start | bytes 1572872 | tf_op jit(solution)/shard_map/ppermute | solution.py:127
  21.4 15.8 %collective-permute-start.6 = (bf16[256,1024]{1,0:T(8,128)(2,1)}, bf16[256,1024]{1,0:T(8,128)(2,1)}, u32[]{:S(2)}, u32[]{:S(2)}) collective-permute-start(bf16[256,1024]{1,0:T(8,128)(2,1)} %constant_dynamic-update-slice_fusion.refs_4_), channel_id=1, source_target_pairs={{0,24},{1,25},{2,26},{3,27},{4,28},{5,29},{6,30},{7,31},{8,0},{9,1... | collective-permute-start | bytes 1572872 | tf_op jit(solution)/shard_map/ppermute | solution.py:127
  24.5 15.4 %collective-permute-start.2 = (bf16[256,1024]{1,0:T(8,128)(2,1)S(1)}, bf16[256,1024]{1,0:T(8,128)(2,1)}, u32[]{:S(2)}, u32[]{:S(2)}) collective-permute-start(bf16[256,1024]{1,0:T(8,128)(2,1)S(1)} %pad_maximum_fusion.refs_3_), channel_id=1, source_target_pairs={{0,8},{1,9},{2,10},{3,11},{4,12},{5,13},{6,14},{7,15},{8,16},{9,17... | collective-permute-start | bytes 1572872 | tf_op jit(solution)/shard_map/ppermute | solution.py:127
  25.4 16.1 %collective-permute-start.9 = (bf16[256,1024]{1,0:T(8,128)(2,1)S(1)}, bf16[256,1024]{1,0:T(8,128)(2,1)}, u32[]{:S(2)}, u32[]{:S(2)}) collective-permute-start(bf16[256,1024]{1,0:T(8,128)(2,1)S(1)} %pad_maximum_fusion.1.refs_9_), channel_id=1, source_target_pairs={{0,2},{1,3},{2,4},{3,5},{4,6},{5,7},{6,0},{7,1},{8,10},{9,11},{10,... | collective-permute-start | bytes 1572872 | tf_op jit(solution)/shard_map/ppermute | solution.py:127
  36.0 14.7 %collective-permute-start.15 = (bf16[256,1024]{1,0:T(8,128)(2,1)}, bf16[256,1024]{1,0:T(8,128)(2,1)S(1)}, u32[]{:S(2)}, u32[]{:S(2)}) collective-permute-start(bf16[256,1024]{1,0:T(8,128)(2,1)} %constant_dynamic-update-slice_fusion.refs_4_), channel_id=1, source_target_pairs={{0,8},{1,9},{2,10},{3,11},{4,12},{5,13},{6,14},{7,15},{8,16},{9,17... | collective-permute-start | bytes 1572872 | tf_op jit(solution)/shard_map/ppermute | solution.py:127
  37.3 14.7 %collective-permute-start.17 = (bf16[256,1024]{1,0:T(8,128)(2,1)}, bf16[256,1024]{1,0:T(8,128)(2,1)}, u32[]{:S(2)}, u32[]{:S(2)}) collective-permute-start(bf16[256,1024]{1,0:T(8,128)(2,1)} %constant_dynamic-update-slice_fusion.2.refs_10_), channel_id=1, source_target_pairs={{0,2},{1,3},{2,4},{3,5},{4,6},{5,7},{6,0},{7,1},{8,10},{9,11},{10,... | collective-permute-start | bytes 1572872 | tf_op jit(solution)/shard_map/ppermute | solution.py:127
  39.8 12.8 %collective-permute-start.16 = (bf16[256,1024]{1,0:T(8,128)(2,1)S(1)}, bf16[256,1024]{1,0:T(8,128)(2,1)}, u32[]{:S(2)}, u32[]{:S(2)}) collective-permute-start(bf16[256,1024]{1,0:T(8,128)(2,1)S(1)} %pad_maximum_fusion.refs_3_), channel_id=1, source_target_pairs={{0,24},{1,25},{2,26},{3,27},{4,28},{5,29},{6,30},{7,31},{8,0},{9,1... | collective-permute-start | bytes 1572872 | tf_op jit(solution)/shard_map/ppermute | solution.py:127
  41.4 14.3 %collective-permute-start.18 = (bf16[256,1024]{1,0:T(8,128)(2,1)S(1)}, bf16[256,1024]{1,0:T(8,128)(2,1)}, u32[]{:S(2)}, u32[]{:S(2)}) collective-permute-start(bf16[256,1024]{1,0:T(8,128)(2,1)S(1)} %pad_maximum_fusion.1.refs_9_), channel_id=1, source_target_pairs={{0,6},{1,7},{2,0},{3,1},{4,2},{5,3},{6,4},{7,5},{8,14},{9,15},{10,... | collective-permute-start | bytes 1572872 | tf_op jit(solution)/shard_map/ppermute | solution.py:127
  51.5 23.5 %collective-permute-start.21 = (bf16[128,4096]{1,0:T(8,128)(2,1)}, bf16[128,4096]{1,0:T(8,128)(2,1)}, u32[]{:S(2)}, u32[]{:S(2)}) collective-permute-start(bf16[128,4096]{1,0:T(8,128)(2,1)} %r_own.1), channel_id=1, source_target_pairs={{0,1},{1,0},{2,3},{3,2},{4,5},{5,4},{6,7},{7,6},{8,9},{9,8},{10,11... | collective-permute-start | bytes 3145736 | tf_op jit(solution)/shard_map/ppermute | solution.py:127
  52.0 16.0 %collective-permute-start.14 = (bf16[256,1024]{1,0:T(8,128)(2,1)}, bf16[256,1024]{1,0:T(8,128)(2,1)}, u32[]{:S(2)}, u32[]{:S(2)}) collective-permute-start(bf16[256,1024]{1,0:T(8,128)(2,1)} %collective-permute-done.13.refs_14_), channel_id=1, source_target_pairs={{0,6},{1,7},{2,0},{3,1},{4,2},{5,3},{6,4},{7,5},{8,14},{9,15},{10,... | collective-permute-start | bytes 1572872 | tf_op jit(solution)/shard_map/ppermute | solution.py:127
  52.6 15.4 %collective-permute-start.7 = (bf16[256,1024]{1,0:T(8,128)(2,1)}, bf16[256,1024]{1,0:T(8,128)(2,1)}, u32[]{:S(2)}, u32[]{:S(2)}) collective-permute-start(bf16[256,1024]{1,0:T(8,128)(2,1)} %collective-permute-done.6.refs_8_), channel_id=1, source_target_pairs={{0,24},{1,25},{2,26},{3,27},{4,28},{5,29},{6,30},{7,31},{8,0},{9,1... | collective-permute-start | bytes 1572872 | tf_op jit(solution)/shard_map/ppermute | solution.py:127
  55.7 12.4 %collective-permute-start.10 = (bf16[256,1024]{1,0:T(8,128)(2,1)}, bf16[256,1024]{1,0:T(8,128)(2,1)}, u32[]{:S(2)}, u32[]{:S(2)}) collective-permute-start(bf16[256,1024]{1,0:T(8,128)(2,1)} %collective-permute-done.9.refs_11_), channel_id=1, source_target_pairs={{0,2},{1,3},{2,4},{3,5},{4,6},{5,7},{6,0},{7,1},{8,10},{9,11},{10,... | collective-permute-start | bytes 1572872 | tf_op jit(solution)/shard_map/ppermute | solution.py:127
  57.1 14.1 %collective-permute-start.3 = (bf16[256,1024]{1,0:T(8,128)(2,1)}, bf16[256,1024]{1,0:T(8,128)(2,1)}, u32[]{:S(2)}, u32[]{:S(2)}) collective-permute-start(bf16[256,1024]{1,0:T(8,128)(2,1)} %collective-permute-done.2.refs_5_), channel_id=1, source_target_pairs={{0,8},{1,9},{2,10},{3,11},{4,12},{5,13},{6,14},{7,15},{8,16},{9,17... | collective-permute-start | bytes 1572872 | tf_op jit(solution)/shard_map/ppermute | solution.py:127
  99.2 14.7 %collective-permute-start.22 = (bf16[16,128,128]{2,1,0:T(8,128)(2,1)}, bf16[16,128,128]{2,1,0:T(8,128)(2,1)S(1)}, u32[]{:S(2)}, u32[]{:S(2)}) collective-permute-start(bf16[16,128,128]{2,1,0:T(8,128)(2,1)} %bitcast.20), channel_id=1, source_target_pairs={{0,32},{32,64},{64,96},{96,0},{1,33},{33,65},{65,97},{97,1},{2,34}... | collective-permute-start | bytes 1572872 | tf_op jit(solution)/shard_map/ppermute | solution.py:308
  100.5 14.5 %collective-permute-start.24 = (bf16[16,128,128]{2,1,0:T(8,128)(2,1)}, bf16[16,128,128]{2,1,0:T(8,128)(2,1)S(1)}, u32[]{:S(2)}, u32[]{:S(2)}) collective-permute-start(bf16[16,128,128]{2,1,0:T(8,128)(2,1)} %bitcast.21), channel_id=1, source_target_pairs={{0,96},{32,0},{64,32},{96,64},{1,97},{33,1},{65,33},{97,65},{2,98}... | collective-permute-start | bytes 1572872 | tf_op jit(solution)/shard_map/ppermute | solution.py:308
  102.2 14.8 %all-to-all-start.1 = ((s32[128,1,384]{2,1,0:T(1,128)}), s32[128,1,384]{2,1,0:T(1,128)S(1)}, u32[]{:S(2)}, u32[]{:S(2)}) async-start(s32[128,1,384]{2,1,0:T(1,128)} %all_to_all.10), calls=%async_computation.1 | async-start | bytes 393216 | tf_op jit(solution)/shard_map/all_to_all | solution.py:334
  109.9 23.0 %collective-permute-start.26 = (bf16[16,128,128]{2,1,0:T(8,128)(2,1)}, bf16[16,128,128]{2,1,0:T(8,128)(2,1)}, u32[]{:S(2)}, u32[]{:S(2)}) collective-permute-start(bf16[16,128,128]{2,1,0:T(8,128)(2,1)} %bitcast.21), channel_id=1, source_target_pairs={{0,32},{32,64},{64,96},{96,0},{1,33},{33,65},{65,97},{97,1},{2,34}... | collective-permute-start | bytes 1572872 | tf_op jit(solution)/shard_map/ppermute | solution.py:308
  111.2 21.7 %collective-permute-start.27 = (bf16[16,128,128]{2,1,0:T(8,128)(2,1)}, bf16[16,128,128]{2,1,0:T(8,128)(2,1)}, u32[]{:S(2)}, u32[]{:S(2)}) collective-permute-start(bf16[16,128,128]{2,1,0:T(8,128)(2,1)} %bitcast.20), channel_id=1, source_target_pairs={{0,96},{32,0},{64,32},{96,64},{1,97},{33,1},{65,33},{97,65},{2,98}... | collective-permute-start | bytes 1572872 | tf_op jit(solution)/shard_map/ppermute | solution.py:308
  113.9 28.2 %collective-permute-start.23 = (bf16[16,128,128]{2,1,0:T(8,128)(2,1)S(1)}, bf16[16,128,128]{2,1,0:T(8,128)(2,1)S(1)}, u32[]{:S(2)}, u32[]{:S(2)}) collective-permute-start(bf16[16,128,128]{2,1,0:T(8,128)(2,1)S(1)} %collective-permute-done.22.refs_0_), channel_id=1, source_target_pairs={{0,32},{32,64},{64,96},{96,0},{1,33},{33,65},{65,97},{97,1},{2,34}... | collective-permute-start | bytes 1572872 | tf_op jit(solution)/shard_map/ppermute | solution.py:308
  115.1 27.0 %collective-permute-start.25 = (bf16[16,128,128]{2,1,0:T(8,128)(2,1)S(1)}, bf16[16,128,128]{2,1,0:T(8,128)(2,1)}, u32[]{:S(2)}, u32[]{:S(2)}) collective-permute-start(bf16[16,128,128]{2,1,0:T(8,128)(2,1)S(1)} %collective-permute-done.24.refs_1_), channel_id=1, source_target_pairs={{0,96},{32,0},{64,32},{96,64},{1,97},{33,1},{65,33},{97,65},{2,98}... | collective-permute-start | bytes 1572872 | tf_op jit(solution)/shard_map/ppermute | solution.py:308
  (23 other events, 291.7 us)
